TPU v7x, 256 devices: a whole 4x4x8 slice. The times are simulated.
256 devices in a mesh: dp: 16 (over x, y_hi, core), tile: 16 (over z, y_lo).
Axes of the slice: x: 4, y: 4 (y_hi: 2, y_lo: 2; y = y_hi * 2 + y_lo), z: 8, core: 2. Of those that a mesh axis runs over, the one named last changes fastest.
Arguments:
- frames: bfloat16 [16, 3, 16, 16, 2048], P('tile', None, None, None, 'dp'), may hold values from -9 to 9
- weights: bfloat16 [16, 64, 8, 972], P('tile'), may hold values from -0.1875 to 0.1875
- connect: int32 [16, 64, 8, 3], P('tile'), may hold values 0 or 1
Outputs:
- update: bfloat16 [16, 64, 8, 972], P('tile')
- loss_value: float32 [], replicated
All inputs are finite; a program needn't handle non-finite values. No bound on the sum of `connect` on one device may be relied on, other than what follows from the above.
Results may differ from a plain program's by a relative error of at most 0.008.
Values may be sent and summed in bfloat16 or wider, within the bound.
A program may use at most 64 MiB of HBM per device.

v0:
```python
import functools
import math

import jax
import jax.numpy as jnp
from jax import lax
from jax.sharding import Mesh
from jax.sharding import PartitionSpec as P

FIELD = 18
MAPS = 8
STRIDE = 2
TILE_PX = 16
INPUTS = 972
HALO = 16
POS = 64
TILE = ("tile_0", "tile_1")
DP_TILE = ("dp_0", "dp_1", "dp_2", "tile_0", "tile_1")
DP = ("dp_0", "dp_1", "dp_2")


sparsity_weight = 1.0
smooth_eps = 0.01
guard_eps = 1e-06


def from_behind(value, axis, steps):
    count = lax.axis_size(axis)
    pairs = [(source, (source + steps) % count) for source in range(count)]
    return lax.ppermute(value, axis, pairs)


def one_axis_at_a_time(x, axes):
    return functools.reduce(lax.psum, axes, x)


def cut_along(x, dim, peers):
    lengths = x.shape
    pieces = x.reshape(*lengths[:dim], peers, lengths[dim] // peers, *lengths[dim + 1 :])
    return jnp.moveaxis(pieces, dim, 0)


def sent_and_summed(x, axis, dim):
    peers = lax.axis_size(axis)
    pieces = lax.all_to_all(cut_along(x, dim, peers), axis, 0, 0, tiled=True)
    return jnp.sum(pieces, axis=0)


def from_everyone(x, axis):
    peers = lax.axis_size(axis)
    return lax.all_to_all(jnp.broadcast_to(x[None], (peers, *x.shape)), axis, 0, 0, tiled=True)


def laid_out(pieces, dim):
    pieces = jnp.moveaxis(pieces, 0, dim)
    lengths = pieces.shape
    return pieces.reshape(*lengths[:dim], lengths[dim] * lengths[dim + 1], *lengths[dim + 2 :])


def gather_directly(x, axis, dim):
    pieces = from_everyone(x, axis)
    return laid_out(pieces, dim)


def masked(values, connect):
    blocked = values.reshape(values.shape[0], values.shape[1], MAPS, 3, FIELD * FIELD)
    opened = connect.astype(values.dtype)[..., None]
    return (blocked * opened).reshape(values.shape)


def patch_block(extended, row_index):
    strip_rows = lax.dynamic_slice_in_dim(extended, row_index * STRIDE, FIELD, 1)
    pieces = [
        strip_rows[:, :, column * STRIDE : column * STRIDE + FIELD]
        for column in range(TILE_PX // STRIDE)
    ]
    blocks = jnp.stack(pieces, 0)
    return blocks.reshape(blocks.shape[0], INPUTS, blocks.shape[-1])


def spread(coeffs, span_px):
    shaped = coeffs.reshape(coeffs.shape[0], 3, FIELD, FIELD, coeffs.shape[-1])
    canvas_strip = jnp.zeros((3, FIELD, span_px, coeffs.shape[-1]), jnp.float32)
    for column in range(TILE_PX // STRIDE):
        canvas_strip = canvas_strip.at[:, :, column * STRIDE : column * STRIDE + FIELD].add(
            shaped[column]
        )
    return canvas_strip


def extend(frame_tile, side_tiles):
    from_right = from_behind(frame_tile, TILE, -1)
    wide_tile = jnp.concatenate([frame_tile, from_right], axis=2)
    from_below = from_behind(wide_tile, TILE, -side_tiles)
    return jnp.concatenate([wide_tile, from_below], axis=1)


def fold_spill(canvas_part, side_tiles):
    from_above = from_behind(
        canvas_part[:, TILE_PX:].astype(jnp.bfloat16), TILE, side_tiles
    ).astype(jnp.float32)
    upper_rows = canvas_part[:, :TILE_PX].at[:, :HALO].add(from_above)
    from_left = from_behind(upper_rows[:, :, TILE_PX:], TILE, 1)
    return upper_rows[:, :, :TILE_PX].at[:, :, :HALO].add(from_left)


def local(frames, weights, connect):
    batch_cols = frames.shape[-1]
    side_tiles = math.isqrt(lax.axis_size(TILE))
    rows_out = TILE_PX // STRIDE
    span_px = TILE_PX + HALO
    effective = masked(weights, connect)[0].reshape(rows_out, rows_out, MAPS, INPUTS)
    frame_tile = frames[0]
    ext_frames = extend(frame_tile, side_tiles)

    def encode_row(canvas_part, row_index):
        blocks = patch_block(ext_frames, row_index)
        w_row = effective[row_index]
        coded = jnp.einsum("cmk,ckb->cmb", w_row, blocks, preferred_element_type=jnp.float32)
        rounded = coded.astype(jnp.bfloat16)
        decoded = jnp.einsum("cmk,cmb->ckb", w_row, rounded, preferred_element_type=jnp.float32)
        start = row_index * STRIDE
        window = lax.dynamic_slice_in_dim(canvas_part, start, FIELD, 1)
        canvas_part = lax.dynamic_update_slice_in_dim(
            canvas_part, window + spread(decoded, span_px), start, 1
        )
        return (canvas_part, coded)

    canvas_part, coded_all = lax.scan(
        encode_row,
        jnp.zeros((3, span_px, span_px, batch_cols), jnp.float32),
        jnp.arange(rows_out, dtype=jnp.int32),
    )
    own_recon = fold_spill(canvas_part, side_tiles)
    errors = own_recon - frame_tile.astype(jnp.float32)
    error_sq = jnp.sum(errors * errors)
    sparse = jnp.sum(jnp.sqrt(smooth_eps + coded_all * coded_all))
    ext_errors = extend(errors.astype(jnp.bfloat16), side_tiles)

    def grad_row(inner, pair):
        row_index, coded = pair
        frame_block = patch_block(ext_frames, row_index)
        error_block = patch_block(ext_errors, row_index)
        w_row = effective[row_index]
        encoded_err = jnp.einsum(
            "cmk,ckb->cmb", w_row, error_block, preferred_element_type=jnp.float32
        )
        left_coef = (2.0 * coded).astype(jnp.bfloat16)
        right_coef = (
            2.0 * encoded_err + sparsity_weight * coded / jnp.sqrt(smooth_eps + coded * coded)
        ).astype(jnp.bfloat16)
        result = jnp.einsum(
            "cmb,ckb->cmk", left_coef, error_block, preferred_element_type=jnp.float32
        )
        result = result + jnp.einsum(
            "cmb,ckb->cmk", right_coef, frame_block, preferred_element_type=jnp.float32
        )
        return (inner, result)

    inner, grad_rows = lax.scan(
        grad_row, jnp.zeros((), jnp.float32), (jnp.arange(rows_out, dtype=jnp.int32), coded_all)
    )
    gradients = masked(grad_rows.reshape(1, POS, MAPS, INPUTS), connect)[0]
    entries = lax.axis_size(TILE) * POS * MAPS * INPUTS
    error_tot, sparse_tot = (
        one_axis_at_a_time(error_sq, DP_TILE),
        one_axis_at_a_time(sparse, DP_TILE),
    )
    shares = sent_and_summed(gradients, DP, 0)
    square = jnp.sum(shares * shares)
    square = one_axis_at_a_time(square, DP_TILE)
    factor = lax.rsqrt(square / entries + guard_eps)
    pieces = (-(shares * factor)).astype(jnp.bfloat16)
    update = gather_directly(pieces, DP, 0)
    loss_value = (error_tot + sparsity_weight * sparse_tot) / (batch_cols * lax.axis_size(DP))
    return (update[None], loss_value)


def solution(mesh):
    torus = Mesh(mesh.devices.reshape(4, 2, 2, 8, 2), ("dp_0", "dp_1", "dp_2", "tile_0", "tile_1"))
    in_specs = (P(TILE, None, None, None, DP), P(TILE, None, None, None), P(TILE, None, None, None))
    out_specs = (P(TILE, None, None, None), P())
    return jax.shard_map(local, mesh=torus, in_specs=in_specs, out_specs=out_specs, check_vma=False)
```

profile of v0, /device:TPU:1, one launch (start us, length us, event | category | flops | bytes accessed | tf_op | source)
XLA Modules:
  0.0 989.8 jit_solution(3565611606355210161)
XLA Ops:
  0.6 7.5 collective-permute-start
  20.0 10.2 %collective-permute-done.1 = bf16[3,16,32,128]{3,2,1,0:T(8,128)(2,1)} collective-permute-done((bf16[3,16,32,128]{3,2,1,0:T(8,128)(2,1)S(1)}, bf16[3,16,32,128]{3,2,1,0:T(8,128)(2,1)}, u32[]{:S(2)}, u32[]{:S(2)}) %collective-permute-start.1) | collective-permute-done | bytes 393248 | tf_op jit(solution)/shard_map/ppermute | solution.py:30
  32.7 477.2 %while.37 = (s32[]{:T(128)}, f32[3,32,32,128]{3,2,1,0:T(8,128)}, f32[8,8,8,128]{3,2,1,0:T(8,128)}, s32[8]{0:T(128)S(1)}, bf16[8,8,8,972]{3,2,1,0:T(8,128)(2,1)},...) while((s32[]{:T(128)}, f32[3,32,32,128]{3,2,1,0:T(8,128)}, ...), condition=%wide.region_1.0_spmd, body=%wide.region_0.1_spmd.sunk | while | flops 32950800 | bytes 56633848 | solution.py:129
  45.7 6.0 scatter-add.54
  52.9 6.0 scatter-add.57
  60.1 6.0 scatter-add.60
  67.3 5.1 scatter-add.61
  73.5 5.1 scatter-add.62
  79.8 5.1 scatter-add.63
  85.0 5.1 scatter-add.64
  105.4 6.0 scatter-add.54
  112.6 6.0 scatter-add.57
  119.8 6.0 scatter-add.60
  127.0 5.1 scatter-add.61
  133.2 5.1 scatter-add.62
  139.5 5.1 scatter-add.63
  144.7 5.1 scatter-add.64
  165.0 6.0 scatter-add.54
  172.2 6.0 scatter-add.57
  179.4 6.0 scatter-add.60
  186.6 5.1 scatter-add.61
  192.9 5.1 scatter-add.62
  204.3 5.1 scatter-add.64
  224.6 6.0 scatter-add.54
  231.8 6.0 scatter-add.57
  239.1 6.0 scatter-add.60
  246.2 5.1 scatter-add.61
  252.5 5.1 scatter-add.62
  258.8 5.1 scatter-add.63
  284.3 6.0 scatter-add.54
  291.5 6.0 scatter-add.57
  298.7 6.0 scatter-add.60
  305.9 5.1 scatter-add.61
  312.1 5.1 scatter-add.62
  318.4 5.1 scatter-add.63
  323.6 5.1 scatter-add.64
  343.9 6.0 scatter-add.54
  351.1 6.0 scatter-add.57
  358.3 6.0 scatter-add.60
  365.5 5.1 scatter-add.61
  371.8 5.1 scatter-add.62
  378.0 5.1 scatter-add.63
  383.3 5.1 scatter-add.64
  403.6 6.0 scatter-add.54
  410.8 6.0 scatter-add.57
  418.0 6.0 scatter-add.60
  437.7 5.1 scatter-add.63
  463.2 6.0 scatter-add.54
  470.4 6.0 scatter-add.57
  477.6 6.0 scatter-add.60
  502.6 5.1 scatter-add.64
  514.1 8.5 collective-permute-done.2
  523.9 7.3 collective-permute-start.3
  531.2 9.4 collective-permute-done.3
  541.4 7.0 collective-permute-start.4
  562.2 307.3 %while.38 = (s32[]{:T(128)}, f32[8,8,8,972]{3,2,1,0:T(8,128)}, f32[8,8,8,128]{3,2,1,0:T(8,128)}, s32[8]{0:T(128)S(1)}, bf16[3,32,32,128]{3,2,1,0:T(8,128)(2,1)S(...) while((s32[]{:T(128)}, f32[8,8,8,972]{3,2,1,0:T(8,128)}, ...), condition=%wide.region_3.0_spmd, body=%wide.region_2.0_spmd.sunk | while | flops 47903504 | bytes 60725572 | solution.py:160
  873.7 9.9 %all-to-all-start = ((f32[16,4,8,972]{3,2,1,0:T(8,128)}), f32[16,4,8,972]{3,2,1,0:T(8,128)S(1)}, u32[]{:S(2)}, u32[]{:S(2)}) async-start(f32[16,4,8,972]{3,2,1,0:T(8,128)} %mul.77), calls=%async_computation | async-start | bytes 4194304 | tf_op jit(solution)/shard_map/all_to_all | solution.py:45
  885.6 26.4 %all-to-all-done = f32[16,4,8,972]{3,2,1,0:T(8,128)S(1)} async-done(((f32[16,4,8,972]{3,2,1,0:T(8,128)}), f32[16,4,8,972]{3,2,1,0:T(8,128)S(1)}, u32[]{:S(2)}, u32[]{:S(2)}) %all-to-all-start) | async-done | bytes 1990688 | tf_op jit(solution)/shard_map/all_to_all | solution.py:45
  912.8 7.3 all-reduce.2
  920.0 5.9 all-reduce.5
  925.9 6.8 all-reduce.4
  932.7 21.7 %all-reduce.1 = (f32[]{:T(128)}, f32[]{:T(128)}) all-reduce(f32[]{:T(128)} %get-tuple-element.335, f32[]{:T(128)} %get-tuple-element.336), channel_id=1, replica_groups=mesh['dp_0'=4,'dp_1'=2,'dp_2'=2,'tile_0'=8,'tile_1'=2] {'tile_0'}, use_global_device_ids=true, to_apply=%region_9.10 | all-reduce | flops 2 | bytes 16 | tf_op jit(solution)/shard_map/psum | solution.py:34
  960.7 9.7 all-to-all-start.1
  971.2 16.5 %all-to-all-done.1 = bf16[16,4,8,972]{3,2,1,0:T(8,128)(2,1)S(1)} async-done(((bf16[16,4,8,972]{3,2,1,0:T(8,128)(2,1)}), bf16[16,4,8,972]{3,2,1,0:T(8,128)(2,1)S(1)}, u32[]{:S(2)}, u32[]{:S(2)}) %all-to-all-start.1) | async-done | bytes 995360 | tf_op jit(solution)/shard_map/all_to_all | solution.py:51
  (917 shorter events, 522.4 us)
Async XLA Ops:
  0.6 11.4 %collective-permute-start = (bf16[3,16,16,128]{3,2,1,0:T(8,128)(2,1)}, bf16[3,16,16,128]{3,2,1,0:T(8,128)(2,1)S(1)}, u32[]{:S(2)}, u32[]{:S(2)}) collective-permute-start(bf16[3,16,16,128]{3,2,1,0:T(8,128)(2,1)} %bitcast.80), channel_id=1, source_target_pairs={{0,15},{1,0},{2,1},{3,2},{4,3},{5,4},{6,5},{7,6},{8,7},{9,8},{10,9... | collective-permute-start | bytes 589832 | tf_op jit(solution)/shard_map/ppermute | solution.py:30
  12.0 5.3 copy-start.20
  13.0 17.2 %collective-permute-start.1 = (bf16[3,16,32,128]{3,2,1,0:T(8,128)(2,1)S(1)}, bf16[3,16,32,128]{3,2,1,0:T(8,128)(2,1)}, u32[]{:S(2)}, u32[]{:S(2)}) collective-permute-start(bf16[3,16,32,128]{3,2,1,0:T(8,128)(2,1)S(1)} %pad_maximum_fusion.2), channel_id=1, source_target_pairs={{0,12},{1,13},{2,14},{3,15},{4,0},{5,1},{6,2},{7,3},{8,4},{9,5},{1... | collective-permute-start | bytes 1179656 | tf_op jit(solution)/shard_map/ppermute | solution.py:30
  17.3 12.9 %copy-start.17 = (bf16[1,3,16,16,128]{4,3,2,1,0:T(8,128)(2,1)S(1)}, bf16[1,3,16,16,128]{4,3,2,1,0:T(8,128)(2,1)}, u32[]{:S(2)}) copy-start(bf16[1,3,16,16,128]{4,3,2,1,0:T(8,128)(2,1)} %param.31) | copy-start | bytes 589828
  17.3 12.9 %copy-start.21 = (bf16[3,16,16,128]{3,2,1,0:T(8,128)(2,1)S(1)}, bf16[3,16,16,128]{3,2,1,0:T(8,128)(2,1)}, u32[]{:S(2)}) copy-start(bf16[3,16,16,128]{3,2,1,0:T(8,128)(2,1)} %copy-done.20) | copy-start | bytes 589828
  509.9 30.7 %copy-start.18 = (bf16[1,3,16,16,128]{4,3,2,1,0:T(8,128)(2,1)S(1)}, bf16[1,3,16,16,128]{4,3,2,1,0:T(8,128)(2,1)}, u32[]{:S(2)}) copy-start(bf16[1,3,16,16,128]{4,3,2,1,0:T(8,128)(2,1)} %param.31) | copy-start | bytes 589828
  511.1 11.5 %collective-permute-start.2 = (bf16[3,16,32,128]{3,2,1,0:T(8,128)(2,1)S(1)}, bf16[3,16,32,128]{3,2,1,0:T(8,128)(2,1)S(1)}, u32[]{:S(2)}, u32[]{:S(2)}) collective-permute-start(bf16[3,16,32,128]{3,2,1,0:T(8,128)(2,1)S(1)} %slice.516), channel_id=1, source_target_pairs={{0,4},{1,5},{2,6},{3,7},{4,8},{5,9},{6,10},{7,11},{8,12},{9,13},{1... | collective-permute-start | bytes 1179656 | tf_op jit(solution)/shard_map/ppermute | solution.py:30
  523.9 16.7 %collective-permute-start.3 = (f32[3,16,16,128]{3,2,1,0:T(8,128)S(1)}, f32[3,16,16,128]{3,2,1,0:T(8,128)S(1)}, u32[]{:S(2)}, u32[]{:S(2)}) collective-permute-start(f32[3,16,16,128]{3,2,1,0:T(8,128)S(1)} %slice.499), channel_id=1, source_target_pairs={{0,1},{1,2},{2,3},{3,4},{4,5},{5,6},{6,7},{7,8},{8,9},{9,10},{10,1... | collective-permute-start | bytes 1179656 | tf_op jit(solution)/shard_map/ppermute | solution.py:30
  541.4 10.2 %collective-permute-start.4 = (bf16[3,16,16,128]{3,2,1,0:T(8,128)(2,1)S(1)}, bf16[3,16,16,128]{3,2,1,0:T(8,128)(2,1)S(1)}, u32[]{:S(2)}, u32[]{:S(2)}) collective-permute-start(bf16[3,16,16,128]{3,2,1,0:T(8,128)(2,1)S(1)} %get-tuple-element.382), channel_id=1, source_target_pairs={{0,15},{1,0},{2,1},{3,2},{4,3},{5,4},{6,5},{7,6},{8,7},{9,8},{10,9... | collective-permute-start | bytes 589832 | tf_op jit(solution)/shard_map/ppermute | solution.py:30
  551.6 10.5 %collective-permute-start.5 = (bf16[3,16,32,128]{3,2,1,0:T(8,128)(2,1)S(1)}, bf16[3,16,32,128]{3,2,1,0:T(8,128)(2,1)S(1)}, u32[]{:S(2)}, u32[]{:S(2)}) collective-permute-start(bf16[3,16,32,128]{3,2,1,0:T(8,128)(2,1)S(1)} %pad_maximum_fusion.3), channel_id=1, source_target_pairs={{0,12},{1,13},{2,14},{3,15},{4,0},{5,1},{6,2},{7,3},{8,4},{9,5},{1... | collective-permute-start | bytes 1179656 | tf_op jit(solution)/shard_map/ppermute | solution.py:30
  588.5 3.5 copy-start.16
  589.3 2.7 copy-start.14
  590.1 2.0 copy-start.13
  590.9 1.4 copy-start.10
  590.9 1.5 copy-start.9
  590.9 1.5 copy-start.7
  593.7 1.4 copy-start
  626.9 3.5 copy-start.16
  627.7 2.7 copy-start.14
  628.5 2.0 copy-start.13
  629.3 1.4 copy-start.10
  629.3 1.5 copy-start.9
  629.3 1.5 copy-start.7
  632.2 1.4 copy-start
  665.4 3.5 copy-start.16
  666.1 2.7 copy-start.14
  666.9 2.0 copy-start.13
  667.7 1.4 copy-start.10
  667.7 1.5 copy-start.9
  667.7 1.5 copy-start.7
  670.6 1.4 copy-start
  703.8 3.5 copy-start.16
  704.6 2.7 copy-start.14
  705.3 2.0 copy-start.13
  706.1 1.4 copy-start.10
  706.1 1.5 copy-start.9
  706.1 1.5 copy-start.7
  742.2 3.5 copy-start.16
  743.0 2.7 copy-start.14
  743.8 2.0 copy-start.13
  744.5 1.4 copy-start.10
  744.6 1.5 copy-start.9
  744.6 1.5 copy-start.7
  780.6 3.5 copy-start.16
  781.4 2.7 copy-start.14
  782.2 2.0 copy-start.13
  783.0 1.4 copy-start.10
  783.0 1.5 copy-start.9
  783.0 1.5 copy-start.7
  819.0 3.5 copy-start.16
  819.8 2.7 copy-start.14
  820.6 2.0 copy-start.13
  821.4 1.4 copy-start.10
  821.4 1.5 copy-start.9
  821.4 1.5 copy-start.7
  857.4 3.5 copy-start.16
  858.2 2.7 copy-start.14
  859.0 2.0 copy-start.13
  859.8 1.4 copy-start.10
  859.8 1.5 copy-start.9
  859.8 1.5 copy-start.7
  873.6 9.9 %copy-start.19 = (f32[8,8,8,128]{3,2,1,0:T(8,128)S(1)}, f32[8,8,8,128]{3,2,1,0:T(8,128)}, u32[]{:S(2)}) copy-start(f32[8,8,8,128]{3,2,1,0:T(8,128)} %get-tuple-element.674) | copy-start | bytes 786436
  873.7 38.4 %all-to-all-start = ((f32[16,4,8,972]{3,2,1,0:T(8,128)}), f32[16,4,8,972]{3,2,1,0:T(8,128)S(1)}, u32[]{:S(2)}, u32[]{:S(2)}) async-start(f32[16,4,8,972]{3,2,1,0:T(8,128)} %mul.77), calls=%async_computation | async-start | bytes 4194304 | tf_op jit(solution)/shard_map/all_to_all | solution.py:45
  960.7 27.0 %all-to-all-start.1 = ((bf16[16,4,8,972]{3,2,1,0:T(8,128)(2,1)}), bf16[16,4,8,972]{3,2,1,0:T(8,128)(2,1)S(1)}, u32[]{:S(2)}, u32[]{:S(2)}) async-start(bf16[16,4,8,972]{3,2,1,0:T(8,128)(2,1)} %broadcast_in_dim.32), calls=%async_computation.1 | async-start | bytes 2097152 | tf_op jit(solution)/shard_map/all_to_all | solution.py:51
  (85 other events, 99.5 us)
where the time goes:
time: 998 us; the launch traced here: 990 us
  local copies, waits for them, and re-layouts  657 us (66%)
  waiting for transfers between devices  81.2 us (8%)
  matrix products  73.1 us (7%)
  starting transfers between devices  46.4 us (5%)
  blocking collectives  46.1 us (5%)
  loops' own time  43.6 us (4%)
  other arithmetic  37.7 us (4%)
    scatter-add x64, local copies, waits for them, and re-layouts, spread(): canvas_strip.at[:, :, column * STRIDE:column * STRIDE + FIELD]  306 us
    another operation x216, local copies, waits for them, and re-layouts, patch_block(): blocks = jnp.stack(pieces, 0)  198 us
    psum x5, blocking collectives, one_axis_at_a_time(): return functools.reduce(lax.psum, axes, x)  46.1 us
    another operation x56, local copies, waits for them, and re-layouts  43.8 us
    while x440, local copies, waits for them, and re-layouts  40.9 us
    ppermute x6, waiting for transfers between devices, from_behind(): return lax.ppermute(value, axis, pairs)  38.3 us
    slice x16, local copies, waits for them, and re-layouts, patch_block(): strip_rows[:, :, column * STRIDE:column * STRIDE + FIELD]  32.6 us
    dot_general x8, matrix products, grad_row(): jnp.einsum('cmb,ckb->cmk', right_coef, frame_block, preferred_element_typ...  32.1 us
  transfers between devices with their start and end apart: 8, of which 8 were waited for; matrix products, arithmetic and copies ran while one was open for 1% of the time, Pallas kernels for 0%

commit v1 on v0

v1 whole, which is shorter than its diff:
```python
import functools

import jax
import jax.numpy as jnp
from jax import lax
from jax.experimental import pallas as pl
from jax.experimental.pallas import tpu as pltpu
from jax.sharding import PartitionSpec as P

FIELD = 18
MAPS = 8
INPUTS = 972
POS = 64
PX = 16
BLOCK = 640
BAND = 3 * BLOCK
ROWS = POS * MAPS
WIDE = 1024
GROUPS = 4
MESH = pl.DeviceIdType.MESH
F32 = jnp.float32
BF16 = jnp.bfloat16

smooth_eps = 0.01
guard_eps = 1e-06


def dot(a, b):
    return lax.dot_general(a, b, (((1,), (0,)), ((), ())), preferred_element_type=F32)


def dot_nt(a, b):
    return lax.dot_general(a, b, (((1,), (1,)), ((), ())), preferred_element_type=F32)


def kernel(
    n_dp, n_tile, batch, side,
    frames_ref, w_ref, conn_ref,
    out_ref, loss_ref,
    place, wpad, band, band_t, xext, eext, coded, coded_b, enc, dec,
    right_src, right_in, corner_src, corner_in, below_src, below_in,
    grad, gband, gsend, rs_in, rs_half, rs_parts, gathered,
    squares, scal_a, scal_a_in, scal_b, scal_b_in,
    x_send, x_recv, f_send, f_recv, e_send, e_recv,
    rs1_send, rs1_recv, rs2_send, rs2_recv, a_send, a_recv, ag_send, ag_recv, fw_send, fw_recv,
    b_send, b_recv,
):
    d = lax.axis_index("dp")
    t = lax.axis_index("tile")
    n_chip = n_dp // 2
    core = lax.rem(d, 2)
    chip = lax.div(d, 2)
    left = (d, lax.rem(t + n_tile - 1, n_tile))
    right = (d, lax.rem(t + 1, n_tile))
    above = (d, lax.rem(t + n_tile - side, n_tile))
    below = (d, lax.rem(t + side, n_tile))
    sibling = (d + 1 - 2 * core, t)

    barrier = pltpu.get_barrier_semaphore()

    @pl.loop(1, n_dp)
    def _(o):
        pl.semaphore_signal(barrier, inc=1, device_id=(lax.rem(d + o, n_dp), t), device_id_type=MESH)

    @pl.loop(1, n_tile)
    def _(o):
        pl.semaphore_signal(barrier, inc=1, device_id=(d, lax.rem(t + o, n_tile)), device_id_type=MESH)

    pl.semaphore_wait(barrier, n_dp + n_tile - 2)

    def remote(src, dst, send, recv, device):
        return pltpu.make_async_remote_copy(
            src_ref=src, dst_ref=dst, send_sem=send, recv_sem=recv, device_id=device, device_id_type=MESH
        )

    def halo(own, ext, send, recv):
        def quarter(c, low, far):
            return ext.at[pl.ds(c * 32 + PX * low, PX), pl.ds(PX * far, PX)]

        to_left = [remote(own(c), quarter(c, 0, 1), send.at[c], recv.at[c], left) for c in range(3)]
        to_above = [remote(own(c), quarter(c, 1, 0), send.at[3 + c], recv.at[3 + c], above) for c in range(3)]
        relay = [
            remote(quarter(c, 1, 0), quarter(c, 1, 1), send.at[6 + c], recv.at[6 + c], left)
            for c in range(3)
        ]
        return to_left, to_above, relay

    x_left, x_above, x_relay = halo(lambda c: frames_ref.at[c], xext, x_send, x_recv)
    for c in range(3):
        x_above[c].start()
        x_left[c].start()
    for c in range(3):
        xext[pl.ds(c * 32, PX), pl.ds(0, PX)] = frames_ref[c]

    lane = lax.broadcasted_iota(jnp.int32, (1, BAND), 1)
    chan = jnp.where(lane >= BLOCK, 1, 0) + jnp.where(lane >= 2 * BLOCK, 1, 0)
    spot = lane - BLOCK * chan
    prow = spot >> 5
    pcol = spot & 31
    source = jnp.where((pcol < FIELD) & (prow < FIELD), FIELD * FIELD * chan + FIELD * prow + pcol, -1)

    @pl.loop(0, WIDE // 32)
    def _(b):
        number = lax.broadcasted_iota(jnp.int32, (32, BAND), 0) + b * 32
        place[pl.ds(b * 32, 32), :] = jnp.where(number == source, 1.0, 0.0).astype(BF16)

    wpad[:, pl.ds(896, 128)] = jnp.zeros((128, 128), BF16)

    def open_map(g, c):
        return conn_ref[pl.ds(g * 16, 16), :, c : c + 1].astype(F32).reshape(128, 1)

    @pl.loop(0, GROUPS)
    def _(g):
        wpad[:, pl.ds(0, INPUTS)] = w_ref[pl.ds(g * 16, 16)].astype(F32).reshape(128, INPUTS).astype(BF16)
        for c in range(3):
            lanes = pl.ds(c * BLOCK, BLOCK)
            lo, hi = ((0, 384), (256, 768), (640, 1024))[c]
            spread = dot(wpad[:, lo:hi], place[lo:hi, lanes]) * open_map(g, c)
            rolled = []
            for p in range(16):
                shift = 64 * (p // 8) + 2 * (p % 8)
                part = spread[p * 8 : p * 8 + 8]
                rolled.append(pltpu.roll(part, shift, 1) if shift else part)
            whole = jnp.concatenate(rolled, axis=0)
            band[pl.ds(g * 128, 128), lanes] = whole.astype(BF16)
            band_t[g, lanes, :] = whole.T.astype(BF16)

    def strip(ext, g, c):
        return ext[pl.ds(c * 32 + 4 * g, 20)].reshape(BLOCK, 128)

    for c in range(3):
        x_above[c].wait_recv()
        x_relay[c].start()
    for c in range(3):
        x_left[c].wait_recv()
        x_relay[c].wait_recv()

        @pl.loop(0, GROUPS)
        def _(g):
            rows = pl.ds(g * 128, 128)
            term = dot(band[rows, c * BLOCK : (c + 1) * BLOCK], strip(xext, g, c))
            if c == 0:
                coded[rows] = term
            else:
                total = coded[rows] + term
                coded[rows] = total
                if c == 2:
                    coded_b[rows] = total.astype(BF16)

    fold_corner = [remote(corner_src.at[c], corner_in.at[c], f_send.at[c], f_recv.at[c], right) for c in range(3)]
    fold_right = [remote(right_src.at[c], right_in.at[c], f_send.at[3 + c], f_recv.at[3 + c], right) for c in range(3)]
    fold_below = [remote(below_src.at[c], below_in.at[c], f_send.at[6 + c], f_recv.at[6 + c], below) for c in range(3)]

    dec[...] = jnp.zeros(dec.shape, F32)
    for c in range(3):

        @pl.loop(0, GROUPS)
        def _(g):
            term = dot(band_t[g, c * BLOCK : (c + 1) * BLOCK, :], coded_b[pl.ds(g * 128, 128)])
            dec[pl.ds(c * 32 + 4 * g, 20)] += term.reshape(20, 32, 128)

        corner_src[c] = dec[pl.ds(c * 32 + PX, PX), pl.ds(PX, PX)].astype(BF16)
        fold_corner[c].start()
        right_src[c] = dec[pl.ds(c * 32, PX), pl.ds(PX, PX)].astype(BF16)
    for c in range(3):
        fold_corner[c].wait_recv()
        summed = dec[pl.ds(c * 32 + PX, PX), pl.ds(0, PX)] + corner_in[c].astype(F32)
        below_src[c] = summed.astype(BF16)
        fold_below[c].start()
        fold_right[c].start()

    value = coded[...]
    penalty = jnp.sqrt(smooth_eps + value * value)
    squares[3:] = jnp.zeros((5, 8, 128), F32)
    squares[2] = jnp.sum(penalty.reshape(ROWS // 8, 8, 128), axis=0)

    e_left, e_above, e_relay = halo(lambda c: eext.at[pl.ds(c * 32, PX), pl.ds(0, PX)], eext, e_send, e_recv)
    error_sq = jnp.zeros((16, 128), F32)
    for c in range(3):
        fold_right[c].wait_recv()
        fold_below[c].wait_recv()
        own = pl.ds(c * 32, PX)
        rebuilt = dec[own, pl.ds(0, PX)] + right_in[c].astype(F32) + below_in[c].astype(F32)
        error = rebuilt - frames_ref[c].astype(F32)
        error_sq = error_sq + jnp.sum(error * error, axis=0)
        eext[own, pl.ds(0, PX)] = error.astype(BF16)
        e_above[c].start()
        e_left[c].start()
    squares[1] = error_sq[:8] + error_sq[8:]

    for c in range(3):
        e_above[c].wait_recv()
        e_relay[c].start()
    for c in range(3):
        e_left[c].wait_recv()
        e_relay[c].wait_recv()

        @pl.loop(0, GROUPS)
        def _(g):
            rows = pl.ds(g * 128, 128)
            lanes = slice(c * BLOCK, (c + 1) * BLOCK)
            errors = strip(eext, g, c)
            term = dot(band[rows, lanes], errors)
            if c == 0:
                enc[rows] = term
            else:
                enc[rows] += term
            grad[rows, lanes] = dot_nt(coded_b[rows] * 2, errors)

    def finish(g):
        rows = pl.ds(pl.multiple_of(g * 128, 128), 128)
        value = coded[rows]
        coef = (2.0 * enc[rows] + value * lax.rsqrt(smooth_eps + value * value)).astype(BF16)
        for c in range(3):
            lanes = slice(c * BLOCK, (c + 1) * BLOCK)
            whole = (grad[rows, lanes] + dot_nt(coef, strip(xext, g, c))) * open_map(g, c)
            rolled = []
            for p in range(16):
                shift = 64 * (p // 8) + 2 * (p % 8)
                part = whole[p * 8 : p * 8 + 8]
                rolled.append(pltpu.roll(part, BLOCK - shift, 1) if shift else part)
            gband[:, lanes] = jnp.concatenate(rolled, axis=0).astype(BF16)
        gsend[rows] = dot_nt(gband[...], place[...]).astype(BF16)

    half = ROWS // 2
    piece = half // n_chip
    swap = []
    for s in range(2):
        g = 2 * (1 - core) + s
        finish(g)
        copy = remote(
            gsend.at[pl.ds(pl.multiple_of(g * 128, 128), 128)], rs_in.at[s], rs1_send.at[s], rs1_recv.at[s], sibling
        )
        copy.start()
        swap.append(copy)
    for s in range(2):
        g = 2 * core + s
        finish(g)
    for s in range(2):
        g = 2 * core + s
        swap[s].wait_recv()
        both = gsend[pl.ds(pl.multiple_of(g * 128, 128), 128)].astype(F32) + rs_in[s].astype(F32)
        rs_half[pl.ds(s * 4, 4)] = both.astype(BF16).reshape(4, piece, WIDE)

    scatter = []
    for o in range(1, n_chip):
        to = lax.rem(chip + o, n_chip)
        copy = remote(rs_half.at[to], rs_parts.at[o - 1], rs2_send.at[o - 1], rs2_recv.at[o - 1], (2 * to + core, t))
        copy.start()
        scatter.append(copy)
    share = rs_half[chip].astype(F32)
    for o in range(1, n_chip):
        scatter[o - 1].wait_recv()
        share = share + rs_parts[o - 1].astype(F32)

    def rows_of(k):
        return pl.ds(pl.multiple_of(core * half + k * piece, piece), piece)

    gathered[rows_of(chip)] = share.astype(BF16)
    square = share * share
    folded = square[:, :128]
    for b in range(1, WIDE // 128):
        folded = folded + square[:, b * 128 : (b + 1) * 128]
    squares[0] = jnp.sum(folded.reshape(piece // 8, 8, 128), axis=0)

    scal_a[...] = jnp.sum(squares[...], axis=1)
    to_dp = []
    for o in range(1, n_dp):
        to = lax.rem(d + o, n_dp)
        copy = remote(scal_a, scal_a_in.at[o - 1], a_send.at[o - 1], a_recv.at[o - 1], (to, t))
        copy.start()
        to_dp.append(copy)
    spread_out = []
    own_share = gathered.at[rows_of(chip)]
    for o in range(1, n_chip):
        to = lax.rem(chip + o, n_chip)
        copy = remote(own_share, own_share, ag_send.at[o - 1], ag_recv.at[o - 1], (2 * to + core, t))
        copy.start()
        spread_out.append(copy)
    forward = [remote(own_share, own_share, fw_send.at[0], fw_recv.at[0], sibling)]
    forward[0].start()

    total = scal_a[...]
    for o in range(1, n_dp):
        to_dp[o - 1].wait_recv()
        total = total + scal_a_in[o - 1]
    scal_b[...] = total
    to_tiles = []
    for o in range(1, n_tile):
        to = lax.rem(t + o, n_tile)
        copy = remote(scal_b, scal_b_in.at[o - 1], b_send.at[o - 1], b_recv.at[o - 1], (d, to))
        copy.start()
        to_tiles.append(copy)
    for o in range(1, n_chip):
        origin = lax.rem(chip + n_chip - o, n_chip)
        arrived = gathered.at[rows_of(origin)]
        spread_out[o - 1].wait_recv()
        copy = remote(arrived, arrived, fw_send.at[o], fw_recv.at[o], sibling)
        copy.start()
        forward.append(copy)
    for o in range(1, n_tile):
        to_tiles[o - 1].wait_recv()
        total = total + scal_b_in[o - 1]
    sums = jnp.sum(total, axis=1, keepdims=True)
    factor = lax.rsqrt(sums[0:1] / (n_tile * ROWS * INPUTS) + guard_eps)
    loss_ref[...] = jnp.broadcast_to((sums[1:2] + sums[2:3]) / batch, loss_ref.shape)
    for copy in forward:
        copy.wait_recv()
    out_ref[...] = (-(gathered[...].astype(F32) * factor)).astype(BF16)

    for copies in (
        x_left, x_above, x_relay, fold_corner, fold_right, fold_below, e_left, e_above, e_relay,
        swap, scatter, to_dp, spread_out, forward, to_tiles,
    ):
        for copy in copies:
            copy.wait_send()


def local(n_dp, n_tile, side, frames, weights, connect):
    n_chip = n_dp // 2
    batch = frames.shape[-1] * n_dp
    dma = pltpu.SemaphoreType.DMA
    vmem = pl.BlockSpec(memory_space=pltpu.VMEM)
    tile = (3, PX, PX, 128)
    scratch = [
        pltpu.VMEM((WIDE, BAND), BF16),
        pltpu.VMEM((128, WIDE), BF16),
        pltpu.VMEM((ROWS, BAND), BF16),
        pltpu.VMEM((GROUPS, BAND, 128), BF16),
        pltpu.VMEM((96, 32, 128), BF16),
        pltpu.VMEM((96, 32, 128), BF16),
        pltpu.VMEM((ROWS, 128), F32),
        pltpu.VMEM((ROWS, 128), BF16),
        pltpu.VMEM((ROWS, 128), F32),
        pltpu.VMEM((96, 32, 128), F32),
        *[pltpu.VMEM(tile, BF16) for _ in range(6)],
        pltpu.VMEM((ROWS, BAND), F32),
        pltpu.VMEM((128, BAND), BF16),
        pltpu.VMEM((ROWS, WIDE), BF16),
        pltpu.VMEM((2, 128, WIDE), BF16),
        pltpu.VMEM((n_chip, ROWS // n_dp, WIDE), BF16),
        pltpu.VMEM((n_chip - 1, ROWS // n_dp, WIDE), BF16),
        pltpu.VMEM((ROWS, WIDE), BF16),
        pltpu.VMEM((8, 8, 128), F32),
        pltpu.VMEM((8, 128), F32),
        pltpu.VMEM((n_dp - 1, 8, 128), F32),
        pltpu.VMEM((8, 128), F32),
        pltpu.VMEM((n_tile - 1, 8, 128), F32),
        *[dma((9,)) for _ in range(6)],
        dma((2,)), dma((2,)),
        dma((n_chip - 1,)), dma((n_chip - 1,)),
        dma((n_dp - 1,)), dma((n_dp - 1,)),
        dma((n_chip - 1,)), dma((n_chip - 1,)),
        dma((n_chip,)), dma((n_chip,)),
        dma((n_tile - 1,)), dma((n_tile - 1,)),
    ]
    update, loss = pl.pallas_call(
        functools.partial(kernel, n_dp, n_tile, batch, side),
        out_shape=(
            jax.ShapeDtypeStruct((ROWS, WIDE), BF16),
            jax.ShapeDtypeStruct((8, 128), F32),
        ),
        in_specs=[vmem] * 3,
        out_specs=(vmem, vmem),
        scratch_shapes=scratch,
        compiler_params=pltpu.CompilerParams(
            collective_id=0, has_side_effects=True, vmem_limit_bytes=48 * 1024 * 1024
        ),
    )(frames[0], weights[0], connect[0])
    return update[:, :INPUTS].reshape(1, POS, MAPS, INPUTS), loss[0, 0]


def solution(mesh):
    n_dp, n_tile = mesh.shape["dp"], mesh.shape["tile"]
    side = int(round(n_tile ** 0.5))
    in_specs = (P("tile", None, None, None, "dp"), P("tile", None, None, None), P("tile", None, None, None))
    out_specs = (P("tile", None, None, None), P())
    return jax.shard_map(
        functools.partial(local, n_dp, n_tile, side), mesh=mesh, in_specs=in_specs, out_specs=out_specs, check_vma=False
    )
```

time: 998 us -> 97.9 us (0.10)
  local copies, waits for them, and re-layouts: 657 us -> 3.7 us
  Pallas kernels: 0 us -> 93.4 us
  waiting for transfers between devices: 81.2 us -> 0 us
  matrix products: 73.1 us -> 0 us
  starting transfers between devices: 46.4 us -> 0 us
  blocking collectives: 46.1 us -> 0 us
  loops' own time: 43.6 us -> 0 us
  other arithmetic: 37.7 us -> 0 us
    scatter-add x64 -> x0, local copies, waits for them, and re-layouts: 306 us -> none  [spread(): canvas_strip.at[:, :, column * STRIDE:column * STRIDE + FIELD]]
    another operation x272 -> x0, local copies, waits for them, and re-layouts: 242 us -> none  [the longest x216 198 us: patch_block(): blocks = jnp.stack(pieces, 0)]
    pallas_call x0 -> x1, Pallas kernels: none -> 93.4 us  [local(): pl.pallas_call(functools.partial(kernel, n_dp, n_tile, batch, side), out_...]
    dot_general x32 -> x0, matrix products: 73.1 us -> none  [the longest x8 32.1 us: grad_row(): jnp.einsum('cmb,ckb->cmk', right_coef, frame_block, preferred_element_typ...]
    psum x5 -> x0, blocking collectives: 46.1 us -> none  [one_axis_at_a_time(): return functools.reduce(lax.psum, axes, x)]
    slice x26 -> x1, local copies, waits for them, and re-layouts: 45.7 us -> 0.51 us  [local(): return (update[:, :INPUTS].reshape(1, POS, MAPS, INPUTS), loss[0, 0])]
    another operation x2 -> x0, loops' own time: 43.6 us -> none  [the longest x1 21.9 us: local(): lax.scan(encode_row, jnp.zeros((3, span_px, span_px, batch_cols), jnp.flo...]
    all_to_all x2 -> x0, waiting for transfers between devices: 42.9 us -> none  [the longest x1 26.4 us: sent_and_summed(): pieces = lax.all_to_all(cut_along(x, dim, peers), axis, 0, 0, tiled=True)]
  transfers between devices with their start and end apart: 8 -> 0, of which waited for: 8 -> 0; matrix products, arithmetic and copies ran while one was open for 1% -> 0% of each run, Pallas kernels for 0% -> 0%
where the time goes in v1:
time: 97.9 us; the launch traced here: 97.8 us
  Pallas kernels  93.4 us (95%)
  local copies, waits for them, and re-layouts  3.7 us (4%)
    pallas_call x1, Pallas kernels, local(): pl.pallas_call(functools.partial(kernel, n_dp, n_tile, batch, side), out_...  93.4 us
    unnamed x5, local copies, waits for them, and re-layouts  2.15 us

profile of v1, /device:TPU:1, one launch (start us, length us, event | category | flops | bytes accessed | tf_op | source)
XLA Modules:
  0.0 97.8 jit_solution(17340501749948560931)
XLA Ops:
  0.6 0.0 copy-start.1
  0.6 0.9 copy.5
  1.6 0.0 copy-done.1
  1.6 0.0 copy-start
  1.6 1.2 %copy-done = bf16[1,64,8,972]{3,2,1,0:T(8,128)(2,1)S(1)} copy-done((bf16[1,64,8,972]{3,2,1,0:T(8,128)(2,1)S(1)}, bf16[1,64,8,972]{3,2,1,0:T(8,128)(2,1)}, u32[]{:S(2)}) %copy-start) | copy-done | bytes 995352
  2.8 93.4 %shard_map.50 = (bf16[512,1024]{1,0:T(8,128)(2,1)S(1)}, f32[8,128]{1,0:T(8,128)S(1)}) custom-call(bf16[3,16,16,128]{3,2,1,0:T(8,128)(2,1)S(1)} %bitcast.8, bf16[64,8,972]{2,1,0:T(8,128)(2,1)S(1)} %bitcast.6, s32[64,8,3]{2,1,0:T(8,128)S(1)} %bitcast.7), custom_call_target="tpu_custom_call" | custom-call | tf_op jit(solution)/shard_map/pallas_call | solution.py:357
  96.2 0.5 slice.7
  96.7 1.0 %slice_bitcast_fusion = bf16[1,64,8,972]{3,2,1,0:T(8,128)(2,1)} fusion(bf16[512,1024]{1,0:T(8,128)(2,1)S(1)} %get-tuple-element.4), kind=kLoop, calls=%fused_computation | loop fusion | bytes 1990656 | tf_op jit(solution)/shard_map/reshape | solution.py:370
Async XLA Ops:
  0.6 0.9 copy-start.1
  1.6 1.2 %copy-start = (bf16[1,64,8,972]{3,2,1,0:T(8,128)(2,1)S(1)}, bf16[1,64,8,972]{3,2,1,0:T(8,128)(2,1)}, u32[]{:S(2)}) copy-start(bf16[1,64,8,972]{3,2,1,0:T(8,128)(2,1)} %param.4) | copy-start | bytes 2985988

commit v2 on v1

v2 whole, which is shorter than its diff:
```python
import functools

import jax
import jax.numpy as jnp
from jax import lax
from jax.experimental import pallas as pl
from jax.experimental.pallas import tpu as pltpu
from jax.sharding import PartitionSpec as P

FIELD = 18
MAPS = 8
INPUTS = 972
POS = 64
PX = 16
BLOCK = 640
BAND = 3 * BLOCK
ROWS = POS * MAPS
WIDE = 1024
GROUPS = 4
MESH = pl.DeviceIdType.MESH
F32 = jnp.float32
BF16 = jnp.bfloat16

smooth_eps = 0.01
guard_eps = 1e-06


def dot(a, b):
    return lax.dot_general(a, b, (((1,), (0,)), ((), ())), preferred_element_type=F32)


def dot_nt(a, b):
    return lax.dot_general(a, b, (((1,), (1,)), ((), ())), preferred_element_type=F32)


def kernel(
    n_dp, n_tile, batch, side,
    frames_ref, w_ref, conn_ref,
    out_ref, loss_ref,
    w_in, opened, place, wpad, band, band_t, xext, eext, coded, coded_b, dec,
    right_src, right_in, corner_src, corner_in, below_src, below_in,
    gband, gsend, rs_in, rs_half, rs_parts, gathered,
    squares, scal, scal_in,
    in_sem, tok,
    x_send, x_recv, f_send, f_recv, e_send, e_recv,
    rs1_send, rs1_recv, rs2_send, rs2_recv, ag_send, ag_recv, fw_send, fw_recv, s_send, s_recv,
):
    d = lax.axis_index("dp")
    t = lax.axis_index("tile")
    n_chip = n_dp // 2
    core = lax.rem(d, 2)
    chip = lax.div(d, 2)
    left = (d, lax.rem(t + n_tile - 1, n_tile))
    right = (d, lax.rem(t + 1, n_tile))
    above = (d, lax.rem(t + n_tile - side, n_tile))
    below = (d, lax.rem(t + side, n_tile))
    sibling = (d + 1 - 2 * core, t)

    def at_chip(k):
        return (2 * k + core, t)

    flips = []
    bit = 1
    while bit < n_chip:
        flips.append(at_chip(chip + bit - 2 * bit * lax.rem(lax.div(chip, bit), 2)))
        bit *= 2

    barrier = pltpu.get_barrier_semaphore()
    greeted = [right, below, sibling, *flips]
    for device in greeted:
        pl.semaphore_signal(barrier, inc=1, device_id=device, device_id_type=MESH)
    own_in = pltpu.make_async_copy(frames_ref, xext.at[:, pl.ds(0, PX), pl.ds(0, PX)], in_sem.at[0])
    own_in.start()
    weights_in = pltpu.make_async_copy(w_ref, w_in, in_sem.at[1])
    weights_in.start()
    pl.semaphore_wait(barrier, len(greeted))

    sent = []

    def remote(src, dst, send, recv, device):
        return pltpu.make_async_remote_copy(
            src_ref=src, dst_ref=dst, send_sem=send, recv_sem=recv, device_id=device, device_id_type=MESH
        )

    def start(copy):
        copy.start()
        sent.append(copy)

    def quarter(ext, low, far, q):
        return ext.at[:, pl.ds(PX * low + 4 * q, 4), pl.ds(PX * far, PX)]

    def halo(own, ext, send, recv):
        to_left = [remote(own(q), quarter(ext, 0, 1, q), send.at[q], recv.at[q], left) for q in range(4)]
        to_above = [remote(own(q), quarter(ext, 1, 0, q), send.at[4 + q], recv.at[4 + q], above) for q in range(4)]
        relay = [
            remote(quarter(ext, 1, 0, q), quarter(ext, 1, 1, q), send.at[8 + q], recv.at[8 + q], left)
            for q in range(4)
        ]
        return to_left, to_above, relay

    x_left, x_above, x_relay = halo(lambda q: frames_ref.at[:, pl.ds(4 * q, 4)], xext, x_send, x_recv)
    start(x_above[0])
    for q in range(4):
        start(x_left[q])
    for q in range(1, 4):
        start(x_above[q])
    for device in flips:
        pl.semaphore_signal(tok.at[0], inc=1, device_id=device, device_id_type=MESH)

    lane = lax.broadcasted_iota(jnp.int32, (1, BAND), 1)
    chan = jnp.where(lane >= BLOCK, 1, 0) + jnp.where(lane >= 2 * BLOCK, 1, 0)
    spot = lane - BLOCK * chan
    prow = spot >> 5
    pcol = spot & 31
    source = jnp.where((pcol < FIELD) & (prow < FIELD), FIELD * FIELD * chan + FIELD * prow + pcol, -1)

    @pl.loop(0, WIDE // 32)
    def _(b):
        number = lax.broadcasted_iota(jnp.int32, (32, BAND), 0) + b * 32
        place[pl.ds(b * 32, 32), :] = jnp.where(number == source, 1.0, 0.0).astype(BF16)

    wpad[:, pl.ds(896, 128)] = jnp.zeros((128, 128), BF16)
    position = lax.broadcasted_iota(jnp.int32, (128, POS), 0) >> 3
    which = lax.broadcasted_iota(jnp.int32, (128, POS), 1)
    spans = ((0, 384), (256, 768), (640, 1024))
    weights_in.wait()

    @pl.loop(0, GROUPS)
    def _(g):
        rows = pl.ds(g * 128, 128)
        wpad[:, pl.ds(0, INPUTS)] = w_in[pl.ds(g * 16, 16)].astype(F32).reshape(128, INPUTS).astype(BF16)
        for c in range(3):
            maps = conn_ref[c].astype(F32)
            tall = jnp.concatenate([maps] * 16, axis=0)
            picked = jnp.where(which == position + g * 16, tall, 0.0)
            opened[c, rows] = jnp.broadcast_to(jnp.sum(picked, axis=1, keepdims=True), (128, 128))
            lanes = pl.ds(c * BLOCK, BLOCK)
            lo, hi = spans[c]
            spread = dot(wpad[:, lo:hi], place[lo:hi, lanes]) * opened[c, rows][:, 0:1]
            rolled = []
            for p in range(16):
                shift = 64 * (p // 8) + 2 * (p % 8)
                part = spread[p * 8 : p * 8 + 8]
                rolled.append(pltpu.roll(part, shift, 1) if shift else part)
            whole = jnp.concatenate(rolled, axis=0)
            band[rows, lanes] = whole.astype(BF16)
            band_t[g, lanes, :] = whole.T.astype(BF16)

    pl.semaphore_wait(tok.at[0], len(flips))
    for device in flips:
        pl.semaphore_signal(tok.at[1], inc=1, device_id=device, device_id_type=MESH)
    dec[...] = jnp.zeros(dec.shape, F32)
    squares[3:] = jnp.zeros((5, 8, 128), F32)
    own_in.wait()

    def strip(ext, g):
        return ext[:, pl.ds(4 * g, 20)].reshape(BAND, 128)

    fold_right = [
        remote(right_src.at[q], right_in.at[q], f_send.at[q], f_recv.at[q], right) for q in range(4)
    ]
    fold_corner = [
        remote(corner_src.at[q], corner_in.at[q], f_send.at[4 + q], f_recv.at[4 + q], right) for q in range(4)
    ]
    fold_below = [
        remote(below_src.at[q], below_in.at[q], f_send.at[8 + q], f_recv.at[8 + q], below) for q in range(4)
    ]
    for g in range(4):
        x_above[g].wait_recv()
        start(x_relay[g])
    for g in range(4):
        x_left[g].wait_recv()
    for g in range(4):
        x_relay[g].wait_recv()
        rows = pl.ds(g * 128, 128)
        value = dot(band[rows, :], strip(xext, g))
        rounded = value.astype(BF16)
        coded[rows] = value
        coded_b[rows] = rounded
        dec[:, pl.ds(4 * g, 20)] += dot(band_t[g], rounded).reshape(3, 20, 32, 128)
        if g < 3:
            right_src[g] = dec[:, pl.ds(4 * g, 4), pl.ds(PX, PX)].astype(BF16)
            start(fold_right[g])
    for q in range(4):
        corner_src[q] = dec[:, pl.ds(PX + 4 * q, 4), pl.ds(PX, PX)].astype(BF16)
        start(fold_corner[q])
    right_src[3] = dec[:, pl.ds(12, 4), pl.ds(PX, PX)].astype(BF16)
    start(fold_right[3])
    for q in range(4):
        fold_corner[q].wait_recv()
        summed = dec[:, pl.ds(PX + 4 * q, 4), pl.ds(0, PX)] + corner_in[q].astype(F32)
        below_src[q] = summed.astype(BF16)
        start(fold_below[q])

    value = coded[...]
    penalty = jnp.sqrt(smooth_eps + value * value)
    squares[2] = jnp.sum(penalty.reshape(ROWS // 8, 8, 128), axis=0)
    pl.semaphore_wait(tok.at[1], len(flips))

    e_left, e_above, e_relay = halo(lambda q: quarter(eext, 0, 0, q), eext, e_send, e_recv)
    error_sq = jnp.zeros((16, 128), F32)
    for q in range(4):
        fold_right[q].wait_recv()
        fold_below[q].wait_recv()
        own = (slice(None), pl.ds(4 * q, 4), pl.ds(0, PX))
        rebuilt = dec[own] + right_in[q].astype(F32) + below_in[q].astype(F32)
        error = rebuilt - xext[own].astype(F32)
        error_sq = error_sq + jnp.sum(error * error, axis=(0, 1))
        eext[own] = error.astype(BF16)
        start(e_above[q])
        start(e_left[q])
        if q > 0:
            e_above[q - 1].wait_recv()
            start(e_relay[q - 1])
    e_above[3].wait_recv()
    start(e_relay[3])
    squares[1] = error_sq[:8] + error_sq[8:]
    for q in range(4):
        e_left[q].wait_recv()

    def finish(g):
        rows = pl.ds(g * 128, 128)
        errors = strip(eext, g)
        value = coded[rows]
        enc = dot(band[rows, :], errors)
        coef = (2.0 * enc + value * lax.rsqrt(smooth_eps + value * value)).astype(BF16)
        both = jnp.concatenate([coded_b[rows] * 2, coef], axis=1)
        parts = []
        for c in range(3):
            lanes = slice(c * BLOCK, (c + 1) * BLOCK)
            patch = jnp.concatenate(
                [ext[c, pl.ds(4 * g, 20)].reshape(BLOCK, 128) for ext in (eext, xext)], axis=1
            )
            whole = dot_nt(both, patch) * opened[c, rows][:, 0:1]
            rolled = []
            for p in range(16):
                shift = 64 * (p // 8) + 2 * (p % 8)
                part = whole[p * 8 : p * 8 + 8]
                rolled.append(pltpu.roll(part, BLOCK - shift, 1) if shift else part)
            gband[...] = jnp.concatenate(rolled, axis=0).astype(BF16)
            lo, hi = spans[c]
            parts.append(dot_nt(gband[...], place[lo:hi, lanes]))
        first, middle, last = parts
        gsend[g, :, 0:256] = first[:, :256].astype(BF16)
        gsend[g, :, 256:384] = (first[:, 256:] + middle[:, :128]).astype(BF16)
        gsend[g, :, 384:640] = middle[:, 128:384].astype(BF16)
        gsend[g, :, 640:768] = (middle[:, 384:] + last[:, :128]).astype(BF16)
        gsend[g, :, 768:1024] = last[:, 128:].astype(BF16)

    def half_of(k):
        return pl.ds(pl.multiple_of(k * 64, 64), 64)

    def lanes_of(k):
        return pl.ds(pl.multiple_of(k * 128, 128), 128)

    swap = [
        remote(gsend.at[g, half_of(1 - core)], rs_in.at[g], rs1_send.at[g], rs1_recv.at[g], sibling)
        for g in range(4)
    ]
    scatter = []

    def combine(batch_no):
        for g in (2 * batch_no, 2 * batch_no + 1):
            swap[g].wait_recv()
            rs_half[g] = (gsend[g, half_of(core)].astype(F32) + rs_in[g].astype(F32)).astype(BF16)
        for o in range(1, n_chip):
            to = lax.rem(chip + o, n_chip)
            n = batch_no * (n_chip - 1) + o - 1
            copy = remote(
                rs_half.at[pl.ds(2 * batch_no, 2), :, lanes_of(to)],
                rs_parts.at[o - 1, pl.ds(2 * batch_no, 2)],
                rs2_send.at[n], rs2_recv.at[n], at_chip(to),
            )
            start(copy)
            scatter.append(copy)

    for g in range(4):
        e_relay[g].wait_recv()
        finish(g)
        start(swap[g])
        if g == 2:
            combine(0)
    combine(1)

    share = rs_half[:, :, lanes_of(chip)].astype(F32)
    for o in range(1, n_chip):
        scatter[o - 1].wait_recv()
        scatter[n_chip - 1 + o - 1].wait_recv()
        share = share + rs_parts[o - 1].astype(F32)

    def place_of(k):
        return gathered.at[:, core, :, lanes_of(k)]

    gathered[:, core, :, lanes_of(chip)] = share.astype(BF16)
    squares[0] = jnp.sum((share * share).reshape(32, 8, 128), axis=0)

    total = jnp.sum(squares[...], axis=1)
    scal[0] = total

    def exchange(stage, targets, first):
        copies = []
        for n, device in enumerate(targets):
            copy = remote(
                scal.at[stage], scal_in.at[first + n], s_send.at[first + n], s_recv.at[first + n], device
            )
            start(copy)
            copies.append(copy)
        return copies

    def collect(total, copies, first):
        for n, copy in enumerate(copies):
            copy.wait_recv()
            total = total + scal_in[first + n]
        return total

    rounds = [
        [at_chip(lax.rem(chip + o, n_chip)) for o in range(1, n_chip)],
        [sibling],
        [(d, lax.rem(t + side * o, n_tile)) for o in range(1, n_tile // side)],
        [(d, t - lax.rem(t, side) + lax.rem(t + o, side)) for o in range(1, side)],
    ]
    copies = exchange(0, rounds[0], 0)
    own_share = place_of(chip)
    spread_out = []
    for o in range(1, n_chip):
        to = lax.rem(chip + o, n_chip)
        copy = remote(own_share, own_share, ag_send.at[o - 1], ag_recv.at[o - 1], at_chip(to))
        start(copy)
        spread_out.append(copy)
    forward = [remote(own_share, own_share, fw_send.at[0], fw_recv.at[0], sibling)]
    start(forward[0])
    first = 0
    for stage in range(1, 4):
        total = collect(total, copies, first)
        first += len(copies)
        scal[stage] = total
        copies = exchange(stage, rounds[stage], first)
    for o in range(1, n_chip):
        origin = lax.rem(chip + n_chip - o, n_chip)
        arrived = place_of(origin)
        spread_out[o - 1].wait_recv()
        copy = remote(arrived, arrived, fw_send.at[o], fw_recv.at[o], sibling)
        start(copy)
        forward.append(copy)
    total = collect(total, copies, first)
    sums = jnp.sum(total, axis=1, keepdims=True)
    factor = lax.rsqrt(sums[0:1] / (n_tile * ROWS * INPUTS) + guard_eps)
    loss_ref[...] = jnp.broadcast_to((sums[1:2] + sums[2:3]) / batch, loss_ref.shape)
    for copy in forward:
        copy.wait_recv()
    out_ref[...] = (-(gathered[...].reshape(ROWS, WIDE).astype(F32) * factor)).astype(BF16)
    for copy in sent:
        copy.wait_send()


def local(n_dp, n_tile, side, frames, weights, connect):
    n_chip = n_dp // 2
    batch = frames.shape[-1] * n_dp
    dma = pltpu.SemaphoreType.DMA
    vmem = pl.BlockSpec(memory_space=pltpu.VMEM)
    hbm = pl.BlockSpec(memory_space=pltpu.HBM)
    n_small = n_chip - 1 + 1 + n_tile // side - 1 + side - 1
    scratch = [
        pltpu.VMEM((POS, MAPS, INPUTS), BF16),
        pltpu.VMEM((3, ROWS, 128), F32),
        pltpu.VMEM((WIDE, BAND), BF16),
        pltpu.VMEM((128, WIDE), BF16),
        pltpu.VMEM((ROWS, BAND), BF16),
        pltpu.VMEM((GROUPS, BAND, 128), BF16),
        pltpu.VMEM((3, 32, 32, 128), BF16),
        pltpu.VMEM((3, 32, 32, 128), BF16),
        pltpu.VMEM((ROWS, 128), F32),
        pltpu.VMEM((ROWS, 128), BF16),
        pltpu.VMEM((3, 32, 32, 128), F32),
        *[pltpu.VMEM((4, 3, 4, PX, 128), BF16) for _ in range(6)],
        pltpu.VMEM((128, BLOCK), BF16),
        pltpu.VMEM((GROUPS, 128, WIDE), BF16),
        pltpu.VMEM((GROUPS, 64, WIDE), BF16),
        pltpu.VMEM((GROUPS, 64, WIDE), BF16),
        pltpu.VMEM((n_chip - 1, GROUPS, 64, 128), BF16),
        pltpu.VMEM((GROUPS, 2, 64, WIDE), BF16),
        pltpu.VMEM((8, 8, 128), F32),
        pltpu.VMEM((4, 8, 128), F32),
        pltpu.VMEM((n_small, 8, 128), F32),
        dma((2,)),
        pltpu.SemaphoreType.REGULAR((2,)),
        *[dma((12,)) for _ in range(6)],
        dma((4,)), dma((4,)),
        dma((2 * (n_chip - 1),)), dma((2 * (n_chip - 1),)),
        dma((n_chip - 1,)), dma((n_chip - 1,)),
        dma((n_chip,)), dma((n_chip,)),
        dma((n_small,)), dma((n_small,)),
    ]
    update, loss = pl.pallas_call(
        functools.partial(kernel, n_dp, n_tile, batch, side),
        out_shape=(
            jax.ShapeDtypeStruct((ROWS, WIDE), BF16),
            jax.ShapeDtypeStruct((8, 128), F32),
        ),
        in_specs=[hbm, hbm, vmem],
        out_specs=(vmem, vmem),
        scratch_shapes=scratch,
        compiler_params=pltpu.CompilerParams(
            collective_id=0, has_side_effects=True, vmem_limit_bytes=63 * 1024 * 1024
        ),
    )(frames[0], weights[0], jnp.transpose(connect[0], (2, 1, 0)))
    return update[:, :INPUTS].reshape(1, POS, MAPS, INPUTS), loss[0, 0]


def solution(mesh):
    n_dp, n_tile = mesh.shape["dp"], mesh.shape["tile"]
    side = int(round(n_tile ** 0.5))
    in_specs = (P("tile", None, None, None, "dp"), P("tile", None, None, None), P("tile", None, None, None))
    out_specs = (P("tile", None, None, None), P())
    return jax.shard_map(
        functools.partial(local, n_dp, n_tile, side), mesh=mesh, in_specs=in_specs, out_specs=out_specs, check_vma=False
    )
```

time: 97.9 us -> 88.9 us (0.908)
  Pallas kernels: 93.4 us -> 84.3 us
    pallas_call x1, Pallas kernels: 93.4 us -> 84.3 us  [local(): pl.pallas_call(functools.partial(kernel, n_dp, n_tile, batch, side), out_...]
    unnamed x5 -> x0, local copies, waits for them, and re-layouts: 2.15 us -> none
    reshape x1, local copies, waits for them, and re-layouts: 1.04 us -> 2.26 us  [local(): return (update[:, :INPUTS].reshape(1, POS, MAPS, INPUTS), loss[0, 0])]
where the time goes in v2:
time: 88.9 us; the launch traced here: 88.4 us
  Pallas kernels  84.3 us (95%)
  local copies, waits for them, and re-layouts  3.45 us (4%)
    pallas_call x1, Pallas kernels, local(): pl.pallas_call(functools.partial(kernel, n_dp, n_tile, batch, side), out_...  84.3 us
    reshape x1, local copies, waits for them, and re-layouts, local(): return (update[:, :INPUTS].reshape(1, POS, MAPS, INPUTS), loss[0, 0])  2.26 us

profile of v2, /device:TPU:1, one launch (start us, length us, event | category | flops | bytes accessed | tf_op | source)
XLA Modules:
  0.0 88.4 jit_solution(14111733454296112789)
XLA Ops:
  0.6 84.3 %shard_map.50 = (bf16[512,1024]{1,0:T(8,128)(2,1)}, f32[8,128]{1,0:T(8,128)}) custom-call(bf16[3,16,16,128]{3,2,1,0:T(8,128)(2,1)} %bitcast.9, bf16[64,8,972]{2,1,0:T(8,128)(2,1)} %bitcast.8, s32[3,8,64]{2,1,0:T(8,128)} %bitcast.10), custom_call_target="tpu_custom_call" | custom-call | tf_op jit(solution)/shard_map/pallas_call | solution.py:394
  85.0 1.2 %slice.7 = f32[1,1]{1,0:T(1,128)} slice(f32[8,128]{1,0:T(8,128)} %get-tuple-element.5), slice={[0:1], [0:1]} | slice | bytes 8 | tf_op jit(solution)/shard_map/slice | solution.py:407
  86.2 2.3 %slice_bitcast_fusion = bf16[1,64,8,972]{3,2,1,0:T(8,128)(2,1)} fusion(bf16[512,1024]{1,0:T(8,128)(2,1)} %get-tuple-element.4), kind=kLoop, calls=%fused_computation | loop fusion | bytes 1990656 | tf_op jit(solution)/shard_map/reshape | solution.py:407

commit v3 on v2

--- a/solution.py
+++ b/solution.py
@@ -39,7 +39,7 @@
     out_ref, loss_ref,
     w_in, opened, place, wpad, band, band_t, xext, eext, coded, coded_b, dec,
     right_src, right_in, corner_src, corner_in, below_src, below_in,
-    gband, gsend, rs_in, rs_half, rs_parts, gathered,
+    x_hold, e_hold, gband, gsend, rs_in, rs_half, rs_parts, gathered,
     squares, scal, scal_in,
     in_sem, tok,
     x_send, x_recv, f_send, f_recv, e_send, e_recv,
@@ -66,7 +66,10 @@
         bit *= 2
 
     barrier = pltpu.get_barrier_semaphore()
-    greeted = [right, below, sibling, *flips]
+    ahead = (d, lax.rem(t + 2, n_tile))
+    behind = (d, lax.rem(t + n_tile - 2, n_tile))
+    odd = lax.rem(t, 2)
+    greeted = [right, below, left, ahead, sibling, *flips]
     for device in greeted:
         pl.semaphore_signal(barrier, inc=1, device_id=device, device_id_type=MESH)
     own_in = pltpu.make_async_copy(frames_ref, xext.at[:, pl.ds(0, PX), pl.ds(0, PX)], in_sem.at[0])
@@ -82,28 +85,46 @@
             src_ref=src, dst_ref=dst, send_sem=send, recv_sem=recv, device_id=device, device_id_type=MESH
         )
 
-    def start(copy):
-        copy.start()
-        sent.append(copy)
+    def start(copy, parity=None):
+        if parity is None:
+            copy.start()
+        else:
+            pl.when(odd == parity)(copy.start)
+        sent.append((copy, parity))
+
+    def start_left(direct, detour):
+        start(direct, 1)
+        start(detour, 0)
+
+    def pass_on(arriving, onward):
+        @pl.when(odd == 1)
+        def _():
+            arriving.wait_recv()
+            onward.start()
+
+        sent.append((onward, 1))
 
     def quarter(ext, low, far, q):
         return ext.at[:, pl.ds(PX * low + 4 * q, 4), pl.ds(PX * far, PX)]
 
-    def halo(own, ext, send, recv):
+    def halo(own, ext, hold, send, recv):
         to_left = [remote(own(q), quarter(ext, 0, 1, q), send.at[q], recv.at[q], left) for q in range(4)]
         to_above = [remote(own(q), quarter(ext, 1, 0, q), send.at[4 + q], recv.at[4 + q], above) for q in range(4)]
         relay = [
             remote(quarter(ext, 1, 0, q), quarter(ext, 1, 1, q), send.at[8 + q], recv.at[8 + q], left)
             for q in range(4)
         ]
-        return to_left, to_above, relay
-
-    x_left, x_above, x_relay = halo(lambda q: frames_ref.at[:, pl.ds(4 * q, 4)], xext, x_send, x_recv)
-    start(x_above[0])
-    for q in range(4):
-        start(x_left[q])
-    for q in range(1, 4):
+        detour = [remote(own(q), hold.at[q], send.at[12 + q], recv.at[12 + q], right) for q in range(4)]
+        onward = [remote(hold.at[q], quarter(ext, 0, 1, q), send.at[16 + q], recv.at[q], behind) for q in range(4)]
+        return to_left, to_above, relay, detour, onward
+
+    x_left, x_above, x_relay, x_detour, x_onward = halo(
+        lambda q: frames_ref.at[:, pl.ds(4 * q, 4)], xext, x_hold, x_send, x_recv
+    )
+    for q in range(4):
         start(x_above[q])
+    for q in range(4):
+        start_left(x_left[q], x_detour[q])
     for device in flips:
         pl.semaphore_signal(tok.at[0], inc=1, device_id=device, device_id_type=MESH)
 
@@ -125,8 +146,7 @@
     spans = ((0, 384), (256, 768), (640, 1024))
     weights_in.wait()
 
-    @pl.loop(0, GROUPS)
-    def _(g):
+    def prepare(g):
         rows = pl.ds(g * 128, 128)
         wpad[:, pl.ds(0, INPUTS)] = w_in[pl.ds(g * 16, 16)].astype(F32).reshape(128, INPUTS).astype(BF16)
         for c in range(3):
@@ -146,6 +166,13 @@
             band[rows, lanes] = whole.astype(BF16)
             band_t[g, lanes, :] = whole.T.astype(BF16)
 
+    prepare(0)
+    for g in range(4):
+        x_above[g].wait_recv()
+        start(x_relay[g])
+        if g < 3:
+            prepare(g + 1)
+        pass_on(x_detour[g], x_onward[g])
     pl.semaphore_wait(tok.at[0], len(flips))
     for device in flips:
         pl.semaphore_signal(tok.at[1], inc=1, device_id=device, device_id_type=MESH)
@@ -165,9 +192,6 @@
     fold_below = [
         remote(below_src.at[q], below_in.at[q], f_send.at[8 + q], f_recv.at[8 + q], below) for q in range(4)
     ]
-    for g in range(4):
-        x_above[g].wait_recv()
-        start(x_relay[g])
     for g in range(4):
         x_left[g].wait_recv()
     for g in range(4):
@@ -197,7 +221,9 @@
     squares[2] = jnp.sum(penalty.reshape(ROWS // 8, 8, 128), axis=0)
     pl.semaphore_wait(tok.at[1], len(flips))
 
-    e_left, e_above, e_relay = halo(lambda q: quarter(eext, 0, 0, q), eext, e_send, e_recv)
+    e_left, e_above, e_relay, e_detour, e_onward = halo(
+        lambda q: quarter(eext, 0, 0, q), eext, e_hold, e_send, e_recv
+    )
     error_sq = jnp.zeros((16, 128), F32)
     for q in range(4):
         fold_right[q].wait_recv()
@@ -208,10 +234,12 @@
         error_sq = error_sq + jnp.sum(error * error, axis=(0, 1))
         eext[own] = error.astype(BF16)
         start(e_above[q])
-        start(e_left[q])
+        start_left(e_left[q], e_detour[q])
         if q > 0:
+            pass_on(e_detour[q - 1], e_onward[q - 1])
             e_above[q - 1].wait_recv()
             start(e_relay[q - 1])
+    pass_on(e_detour[3], e_onward[3])
     e_above[3].wait_recv()
     start(e_relay[3])
     squares[1] = error_sq[:8] + error_sq[8:]
@@ -282,17 +310,46 @@
             combine(0)
     combine(1)
 
-    share = rs_half[:, :, lanes_of(chip)].astype(F32)
-    for o in range(1, n_chip):
-        scatter[o - 1].wait_recv()
-        scatter[n_chip - 1 + o - 1].wait_recv()
-        share = share + rs_parts[o - 1].astype(F32)
-
-    def place_of(k):
-        return gathered.at[:, core, :, lanes_of(k)]
-
-    gathered[:, core, :, lanes_of(chip)] = share.astype(BF16)
-    squares[0] = jnp.sum((share * share).reshape(32, 8, 128), axis=0)
+    def place_of(batch_no, k):
+        return gathered.at[pl.ds(2 * batch_no, 2), core, :, lanes_of(k)]
+
+    spread_out = [[], []]
+    forward = []
+
+    def pass_to_sibling(batch_no, k, o):
+        n = batch_no * n_chip + o
+        block = place_of(batch_no, k)
+        copy = remote(block, block, fw_send.at[n], fw_recv.at[n], sibling)
+        start(copy)
+        forward.append(copy)
+
+    def gather(batch_no):
+        block = place_of(batch_no, chip)
+        for o in range(1, n_chip):
+            n = batch_no * (n_chip - 1) + o - 1
+            to = lax.rem(chip + o, n_chip)
+            copy = remote(block, block, ag_send.at[n], ag_recv.at[n], at_chip(to))
+            start(copy)
+            spread_out[batch_no].append(copy)
+        pass_to_sibling(batch_no, chip, 0)
+
+    def hand_on(batch_no):
+        for o in range(1, n_chip):
+            spread_out[batch_no][o - 1].wait_recv()
+            pass_to_sibling(batch_no, lax.rem(chip + n_chip - o, n_chip), o)
+
+    def add_up(batch_no):
+        pair = pl.ds(2 * batch_no, 2)
+        share = rs_half[pair, :, lanes_of(chip)].astype(F32)
+        for o in range(1, n_chip):
+            scatter[batch_no * (n_chip - 1) + o - 1].wait_recv()
+            share = share + rs_parts[o - 1, pair].astype(F32)
+        gathered[pair, core, :, lanes_of(chip)] = share.astype(BF16)
+        return jnp.sum((share * share).reshape(16, 8, 128), axis=0)
+
+    square = add_up(0)
+    gather(0)
+    squares[0] = square + add_up(1)
 
     total = jnp.sum(squares[...], axis=1)
     scal[0] = total
@@ -315,33 +372,22 @@
 
     rounds = [
         [at_chip(lax.rem(chip + o, n_chip)) for o in range(1, n_chip)],
-        [sibling],
-        [(d, lax.rem(t + side * o, n_tile)) for o in range(1, n_tile // side)],
+        [
+            (d + other * (1 - 2 * core), lax.rem(t + side * o, n_tile))
+            for other in range(2) for o in range(n_tile // side) if other or o
+        ],
         [(d, t - lax.rem(t, side) + lax.rem(t + o, side)) for o in range(1, side)],
     ]
     copies = exchange(0, rounds[0], 0)
-    own_share = place_of(chip)
-    spread_out = []
-    for o in range(1, n_chip):
-        to = lax.rem(chip + o, n_chip)
-        copy = remote(own_share, own_share, ag_send.at[o - 1], ag_recv.at[o - 1], at_chip(to))
-        start(copy)
-        spread_out.append(copy)
-    forward = [remote(own_share, own_share, fw_send.at[0], fw_recv.at[0], sibling)]
-    start(forward[0])
+    gather(1)
+    hand_on(0)
     first = 0
-    for stage in range(1, 4):
+    for stage in range(1, 3):
         total = collect(total, copies, first)
         first += len(copies)
         scal[stage] = total
         copies = exchange(stage, rounds[stage], first)
-    for o in range(1, n_chip):
-        origin = lax.rem(chip + n_chip - o, n_chip)
-        arrived = place_of(origin)
-        spread_out[o - 1].wait_recv()
-        copy = remote(arrived, arrived, fw_send.at[o], fw_recv.at[o], sibling)
-        start(copy)
-        forward.append(copy)
+    hand_on(1)
     total = collect(total, copies, first)
     sums = jnp.sum(total, axis=1, keepdims=True)
     factor = lax.rsqrt(sums[0:1] / (n_tile * ROWS * INPUTS) + guard_eps)
@@ -349,8 +395,11 @@
     for copy in forward:
         copy.wait_recv()
     out_ref[...] = (-(gathered[...].reshape(ROWS, WIDE).astype(F32) * factor)).astype(BF16)
-    for copy in sent:
-        copy.wait_send()
+    for copy, parity in sent:
+        if parity is None:
+            copy.wait_send()
+        else:
+            pl.when(odd == parity)(copy.wait_send)
 
 
 def local(n_dp, n_tile, side, frames, weights, connect):
@@ -359,7 +408,7 @@
     dma = pltpu.SemaphoreType.DMA
     vmem = pl.BlockSpec(memory_space=pltpu.VMEM)
     hbm = pl.BlockSpec(memory_space=pltpu.HBM)
-    n_small = n_chip - 1 + 1 + n_tile // side - 1 + side - 1
+    n_small = n_chip - 1 + 2 * (n_tile // side) - 1 + side - 1
     scratch = [
         pltpu.VMEM((POS, MAPS, INPUTS), BF16),
         pltpu.VMEM((3, ROWS, 128), F32),
@@ -373,6 +422,7 @@
         pltpu.VMEM((ROWS, 128), BF16),
         pltpu.VMEM((3, 32, 32, 128), F32),
         *[pltpu.VMEM((4, 3, 4, PX, 128), BF16) for _ in range(6)],
+        *[pltpu.VMEM((4, 3, 4, PX, 128), BF16) for _ in range(2)],
         pltpu.VMEM((128, BLOCK), BF16),
         pltpu.VMEM((GROUPS, 128, WIDE), BF16),
         pltpu.VMEM((GROUPS, 64, WIDE), BF16),
@@ -384,11 +434,11 @@
         pltpu.VMEM((n_small, 8, 128), F32),
         dma((2,)),
         pltpu.SemaphoreType.REGULAR((2,)),
-        *[dma((12,)) for _ in range(6)],
+        *[dma((20,)) for _ in range(6)],
         dma((4,)), dma((4,)),
         dma((2 * (n_chip - 1),)), dma((2 * (n_chip - 1),)),
-        dma((n_chip - 1,)), dma((n_chip - 1,)),
-        dma((n_chip,)), dma((n_chip,)),
+        dma((2 * (n_chip - 1),)), dma((2 * (n_chip - 1),)),
+        dma((2 * n_chip,)), dma((2 * n_chip,)),
         dma((n_small,)), dma((n_small,)),
     ]
     update, loss = pl.pallas_call(
@@ -401,7 +451,7 @@
         out_specs=(vmem, vmem),
         scratch_shapes=scratch,
         compiler_params=pltpu.CompilerParams(
-            collective_id=0, has_side_effects=True, vmem_limit_bytes=63 * 1024 * 1024
+            collective_id=0, has_side_effects=True, vmem_limit_bytes=54000 * 1024
         ),
     )(frames[0], weights[0], jnp.transpose(connect[0], (2, 1, 0)))
     return update[:, :INPUTS].reshape(1, POS, MAPS, INPUTS), loss[0, 0]

time: 88.9 us -> 85.5 us (0.962)
  Pallas kernels: 84.3 us -> 81.5 us
    pallas_call x1, Pallas kernels: 84.3 us -> 81.5 us  [local(): pl.pallas_call(functools.partial(kernel, n_dp, n_tile, batch, side), out_...]
    unnamed x0 -> x4, local copies, waits for them, and re-layouts: none -> 1.63 us
    reshape x1, local copies, waits for them, and re-layouts: 2.26 us -> 1.04 us  [local(): return (update[:, :INPUTS].reshape(1, POS, MAPS, INPUTS), loss[0, 0])]
where the time goes in v3:
time: 85.5 us; the launch traced here: 85.4 us
  Pallas kernels  81.5 us (95%)
  local copies, waits for them, and re-layouts  3.18 us (4%)
    pallas_call x1, Pallas kernels, local(): pl.pallas_call(functools.partial(kernel, n_dp, n_tile, batch, side), out_...  81.5 us

profile of v3, /device:TPU:1, one launch (start us, length us, event | category | flops | bytes accessed | tf_op | source)
XLA Modules:
  0.0 85.4 jit_solution(12619243991761157711)
XLA Ops:
  0.6 0.0 copy-start
  0.6 0.9 %copy-done = bf16[1,3,16,16,128]{4,3,2,1,0:T(8,128)(2,1)S(1)} copy-done((bf16[1,3,16,16,128]{4,3,2,1,0:T(8,128)(2,1)S(1)}, bf16[1,3,16,16,128]{4,3,2,1,0:T(8,128)(2,1)}, u32[]{:S(2)}) %copy-start) | copy-done | bytes 196632
  1.6 0.0 copy-start.1
  1.6 0.7 copy-done.1
  2.3 81.5 %shard_map.50 = (bf16[512,1024]{1,0:T(8,128)(2,1)S(1)}, f32[8,128]{1,0:T(8,128)S(1)}) custom-call(bf16[3,16,16,128]{3,2,1,0:T(8,128)(2,1)S(1)} %bitcast.8, bf16[64,8,972]{2,1,0:T(8,128)(2,1)} %bitcast.10, s32[3,8,64]{2,1,0:T(8,128)S(1)} %bitcast.9), custom_call_target="tpu_custom_call" | custom-call | tf_op jit(solution)/shard_map/pallas_call | solution.py:444
  83.8 0.5 slice.7
  84.3 1.0 %slice_bitcast_fusion = bf16[1,64,8,972]{3,2,1,0:T(8,128)(2,1)} fusion(bf16[512,1024]{1,0:T(8,128)(2,1)S(1)} %get-tuple-element.4), kind=kLoop, calls=%fused_computation | loop fusion | bytes 1990656 | tf_op jit(solution)/shard_map/reshape | solution.py:457
Async XLA Ops:
  0.6 0.9 %copy-start = (bf16[1,3,16,16,128]{4,3,2,1,0:T(8,128)(2,1)S(1)}, bf16[1,3,16,16,128]{4,3,2,1,0:T(8,128)(2,1)}, u32[]{:S(2)}) copy-start(bf16[1,3,16,16,128]{4,3,2,1,0:T(8,128)(2,1)} %param.3) | copy-start | bytes 589828
  1.6 0.7 copy-start.1

commit v4 on v3

--- a/solution.py
+++ b/solution.py
@@ -58,6 +58,18 @@
 
     def at_chip(k):
         return (2 * k + core, t)
+
+    n_x = n_chip // 2
+    x_at = lax.div(chip, 2)
+    y_at = lax.rem(chip, 2)
+    along_x = sorted(range(n_x), key=lambda o: -min(o, n_x - o))
+    steps = [(dx, 1) for dx in along_x] + [(dx, 0) for dx in along_x if dx]
+
+    def chip_to(step):
+        return 2 * lax.rem(x_at + step[0], n_x) + lax.rem(y_at + step[1], 2)
+
+    def chip_from(step):
+        return 2 * lax.rem(x_at + n_x - step[0], n_x) + lax.rem(y_at + step[1], 2)
 
     flips = []
     bit = 1
@@ -291,8 +303,8 @@
         for g in (2 * batch_no, 2 * batch_no + 1):
             swap[g].wait_recv()
             rs_half[g] = (gsend[g, half_of(core)].astype(F32) + rs_in[g].astype(F32)).astype(BF16)
-        for o in range(1, n_chip):
-            to = lax.rem(chip + o, n_chip)
+        for o, step in enumerate(steps, 1):
+            to = chip_to(step)
             n = batch_no * (n_chip - 1) + o - 1
             copy = remote(
                 rs_half.at[pl.ds(2 * batch_no, 2), :, lanes_of(to)],
@@ -325,18 +337,18 @@
 
     def gather(batch_no):
         block = place_of(batch_no, chip)
-        for o in range(1, n_chip):
+        for o, step in enumerate(steps, 1):
             n = batch_no * (n_chip - 1) + o - 1
-            to = lax.rem(chip + o, n_chip)
+            to = chip_to(step)
             copy = remote(block, block, ag_send.at[n], ag_recv.at[n], at_chip(to))
             start(copy)
             spread_out[batch_no].append(copy)
         pass_to_sibling(batch_no, chip, 0)
 
     def hand_on(batch_no):
-        for o in range(1, n_chip):
+        for o in reversed(range(1, n_chip)):
             spread_out[batch_no][o - 1].wait_recv()
-            pass_to_sibling(batch_no, lax.rem(chip + n_chip - o, n_chip), o)
+            pass_to_sibling(batch_no, chip_from(steps[o - 1]), o)
 
     def add_up(batch_no):
         pair = pl.ds(2 * batch_no, 2)
@@ -371,22 +383,18 @@
         return total
 
     rounds = [
-        [at_chip(lax.rem(chip + o, n_chip)) for o in range(1, n_chip)],
-        [
-            (d + other * (1 - 2 * core), lax.rem(t + side * o, n_tile))
-            for other in range(2) for o in range(n_tile // side) if other or o
-        ],
-        [(d, t - lax.rem(t, side) + lax.rem(t + o, side)) for o in range(1, side)],
+        [(2 * chip_to(step) + lax.rem(core + o, 2), t) for step in steps for o in (1, 0)] + [sibling],
+        [(d, lax.rem(t + o, n_tile)) for o in sorted(range(1, n_tile), key=lambda o: -min(o, n_tile - o))],
     ]
     copies = exchange(0, rounds[0], 0)
     gather(1)
-    hand_on(0)
     first = 0
-    for stage in range(1, 3):
+    for stage in range(1, len(rounds)):
         total = collect(total, copies, first)
         first += len(copies)
         scal[stage] = total
         copies = exchange(stage, rounds[stage], first)
+    hand_on(0)
     hand_on(1)
     total = collect(total, copies, first)
     sums = jnp.sum(total, axis=1, keepdims=True)
@@ -408,7 +416,7 @@
     dma = pltpu.SemaphoreType.DMA
     vmem = pl.BlockSpec(memory_space=pltpu.VMEM)
     hbm = pl.BlockSpec(memory_space=pltpu.HBM)
-    n_small = n_chip - 1 + 2 * (n_tile // side) - 1 + side - 1
+    n_small = n_dp + n_tile - 2
     scratch = [
         pltpu.VMEM((POS, MAPS, INPUTS), BF16),
         pltpu.VMEM((3, ROWS, 128), F32),

time: 85.5 us -> 83.2 us (0.973)
  Pallas kernels: 81.5 us -> 79.2 us
    pallas_call x1, Pallas kernels: 81.5 us -> 79.2 us  [local(): pl.pallas_call(functools.partial(kernel, n_dp, n_tile, batch, side), out_...]
where the time goes in v4:
time: 83.2 us; the launch traced here: 83.1 us
  Pallas kernels  79.2 us (95%)
  local copies, waits for them, and re-layouts  3.18 us (4%)
    pallas_call x1, Pallas kernels, local(): pl.pallas_call(functools.partial(kernel, n_dp, n_tile, batch, side), out_...  79.2 us

profile of v4, /device:TPU:1, one launch (start us, length us, event | category | flops | bytes accessed | tf_op | source)
XLA Modules:
  0.0 83.1 jit_solution(3765844230756099653)
XLA Ops:
  0.6 0.0 copy-start
  0.6 0.9 %copy-done = bf16[1,3,16,16,128]{4,3,2,1,0:T(8,128)(2,1)S(1)} copy-done((bf16[1,3,16,16,128]{4,3,2,1,0:T(8,128)(2,1)S(1)}, bf16[1,3,16,16,128]{4,3,2,1,0:T(8,128)(2,1)}, u32[]{:S(2)}) %copy-start) | copy-done | bytes 196632
  1.6 0.0 copy-start.1
  1.6 0.7 copy-done.1
  2.3 79.2 %shard_map.50 = (bf16[512,1024]{1,0:T(8,128)(2,1)S(1)}, f32[8,128]{1,0:T(8,128)S(1)}) custom-call(bf16[3,16,16,128]{3,2,1,0:T(8,128)(2,1)S(1)} %bitcast.8, bf16[64,8,972]{2,1,0:T(8,128)(2,1)} %bitcast.10, s32[3,8,64]{2,1,0:T(8,128)S(1)} %bitcast.9), custom_call_target="tpu_custom_call" | custom-call | tf_op jit(solution)/shard_map/pallas_call | solution.py:452
  81.5 0.5 slice.7
  82.0 1.0 %slice_bitcast_fusion = bf16[1,64,8,972]{3,2,1,0:T(8,128)(2,1)} fusion(bf16[512,1024]{1,0:T(8,128)(2,1)S(1)} %get-tuple-element.4), kind=kLoop, calls=%fused_computation | loop fusion | bytes 1990656 | tf_op jit(solution)/shard_map/reshape | solution.py:465
Async XLA Ops:
  0.6 0.9 %copy-start = (bf16[1,3,16,16,128]{4,3,2,1,0:T(8,128)(2,1)S(1)}, bf16[1,3,16,16,128]{4,3,2,1,0:T(8,128)(2,1)}, u32[]{:S(2)}) copy-start(bf16[1,3,16,16,128]{4,3,2,1,0:T(8,128)(2,1)} %param.3) | copy-start | bytes 589828
  1.6 0.7 copy-start.1

commit v5 on v4

--- a/solution.py
+++ b/solution.py
@@ -180,11 +180,11 @@
 
     prepare(0)
     for g in range(4):
+        pass_on(x_detour[g], x_onward[g])
         x_above[g].wait_recv()
         start(x_relay[g])
         if g < 3:
             prepare(g + 1)
-        pass_on(x_detour[g], x_onward[g])
     pl.semaphore_wait(tok.at[0], len(flips))
     for device in flips:
         pl.semaphore_signal(tok.at[1], inc=1, device_id=device, device_id_type=MESH)
@@ -249,11 +249,13 @@
         start_left(e_left[q], e_detour[q])
         if q > 0:
             pass_on(e_detour[q - 1], e_onward[q - 1])
-            e_above[q - 1].wait_recv()
-            start(e_relay[q - 1])
+        if q > 1:
+            e_above[q - 2].wait_recv()
+            start(e_relay[q - 2])
     pass_on(e_detour[3], e_onward[3])
-    e_above[3].wait_recv()
-    start(e_relay[3])
+    for q in (2, 3):
+        e_above[q].wait_recv()
+        start(e_relay[q])
     squares[1] = error_sq[:8] + error_sq[8:]
     for q in range(4):
         e_left[q].wait_recv()

time: 83.2 us -> 81.4 us (0.978)
  Pallas kernels: 79.2 us -> 77.4 us
    pallas_call x1, Pallas kernels: 79.2 us -> 77.4 us  [local(): pl.pallas_call(functools.partial(kernel, n_dp, n_tile, batch, side), out_...]
where the time goes in v5:
time: 81.4 us; the launch traced here: 81.2 us
  Pallas kernels  77.4 us (95%)
  local copies, waits for them, and re-layouts  3.18 us (4%)
    pallas_call x1, Pallas kernels, local(): pl.pallas_call(functools.partial(kernel, n_dp, n_tile, batch, side), out_...  77.4 us

profile of v5, /device:TPU:1, one launch (start us, length us, event | category | flops | bytes accessed | tf_op | source)
XLA Modules:
  0.0 81.2 jit_solution(7475771000732507893)
XLA Ops:
  0.6 0.0 copy-start
  0.6 0.9 %copy-done = bf16[1,3,16,16,128]{4,3,2,1,0:T(8,128)(2,1)S(1)} copy-done((bf16[1,3,16,16,128]{4,3,2,1,0:T(8,128)(2,1)S(1)}, bf16[1,3,16,16,128]{4,3,2,1,0:T(8,128)(2,1)}, u32[]{:S(2)}) %copy-start) | copy-done | bytes 196632
  1.6 0.0 copy-start.1
  1.6 0.7 copy-done.1
  2.3 77.4 %shard_map.50 = (bf16[512,1024]{1,0:T(8,128)(2,1)S(1)}, f32[8,128]{1,0:T(8,128)S(1)}) custom-call(bf16[3,16,16,128]{3,2,1,0:T(8,128)(2,1)S(1)} %bitcast.8, bf16[64,8,972]{2,1,0:T(8,128)(2,1)} %bitcast.10, s32[3,8,64]{2,1,0:T(8,128)S(1)} %bitcast.9), custom_call_target="tpu_custom_call" | custom-call | tf_op jit(solution)/shard_map/pallas_call | solution.py:454
  79.6 0.5 slice.7
  80.2 1.0 %slice_bitcast_fusion = bf16[1,64,8,972]{3,2,1,0:T(8,128)(2,1)} fusion(bf16[512,1024]{1,0:T(8,128)(2,1)S(1)} %get-tuple-element.4), kind=kLoop, calls=%fused_computation | loop fusion | bytes 1990656 | tf_op jit(solution)/shard_map/reshape | solution.py:467
Async XLA Ops:
  0.6 0.9 %copy-start = (bf16[1,3,16,16,128]{4,3,2,1,0:T(8,128)(2,1)S(1)}, bf16[1,3,16,16,128]{4,3,2,1,0:T(8,128)(2,1)}, u32[]{:S(2)}) copy-start(bf16[1,3,16,16,128]{4,3,2,1,0:T(8,128)(2,1)} %param.3) | copy-start | bytes 589828
  1.6 0.7 copy-start.1

commit v6 on v5

--- a/solution.py
+++ b/solution.py
@@ -180,11 +180,11 @@
 
     prepare(0)
     for g in range(4):
-        pass_on(x_detour[g], x_onward[g])
         x_above[g].wait_recv()
         start(x_relay[g])
         if g < 3:
             prepare(g + 1)
+        pass_on(x_detour[g], x_onward[g])
     pl.semaphore_wait(tok.at[0], len(flips))
     for device in flips:
         pl.semaphore_signal(tok.at[1], inc=1, device_id=device, device_id_type=MESH)

time: 81.4 us -> 81 us (level)
  no operation moved by 1% of the time
where the time goes in v6:
time: 81 us; the launch traced here: 80.8 us
  Pallas kernels  77 us (95%)
  local copies, waits for them, and re-layouts  3.18 us (4%)
    pallas_call x1, Pallas kernels, local(): pl.pallas_call(functools.partial(kernel, n_dp, n_tile, batch, side), out_...  77 us
    unnamed x4, local copies, waits for them, and re-layouts  1.63 us

profile of v6, /device:TPU:1, one launch (start us, length us, event | category | flops | bytes accessed | tf_op | source)
XLA Modules:
  0.0 80.8 jit_solution(10304137811027757448)
XLA Ops:
  0.6 0.0 copy-start
  0.6 0.9 %copy-done = bf16[1,3,16,16,128]{4,3,2,1,0:T(8,128)(2,1)S(1)} copy-done((bf16[1,3,16,16,128]{4,3,2,1,0:T(8,128)(2,1)S(1)}, bf16[1,3,16,16,128]{4,3,2,1,0:T(8,128)(2,1)}, u32[]{:S(2)}) %copy-start) | copy-done | bytes 196632
  1.6 0.0 copy-start.1
  1.6 0.7 copy-done.1
  2.3 77.0 %shard_map.50 = (bf16[512,1024]{1,0:T(8,128)(2,1)S(1)}, f32[8,128]{1,0:T(8,128)S(1)}) custom-call(bf16[3,16,16,128]{3,2,1,0:T(8,128)(2,1)S(1)} %bitcast.8, bf16[64,8,972]{2,1,0:T(8,128)(2,1)} %bitcast.10, s32[3,8,64]{2,1,0:T(8,128)S(1)} %bitcast.9), custom_call_target="tpu_custom_call" | custom-call | tf_op jit(solution)/shard_map/pallas_call | solution.py:454
  79.3 0.5 slice.7
  79.8 1.0 %slice_bitcast_fusion = bf16[1,64,8,972]{3,2,1,0:T(8,128)(2,1)} fusion(bf16[512,1024]{1,0:T(8,128)(2,1)S(1)} %get-tuple-element.4), kind=kLoop, calls=%fused_computation | loop fusion | bytes 1990656 | tf_op jit(solution)/shard_map/reshape | solution.py:467
Async XLA Ops:
  0.6 0.9 %copy-start = (bf16[1,3,16,16,128]{4,3,2,1,0:T(8,128)(2,1)S(1)}, bf16[1,3,16,16,128]{4,3,2,1,0:T(8,128)(2,1)}, u32[]{:S(2)}) copy-start(bf16[1,3,16,16,128]{4,3,2,1,0:T(8,128)(2,1)} %param.3) | copy-start | bytes 589828
  1.6 0.7 copy-start.1
